TPU v7x, 32 devices: a whole 2x2x4 slice. The times are simulated.
32 devices in a mesh: replica: 4 (over z), shard: 8 (over y, x, core).
Axes of the slice: x: 2, y: 2, z: 4, core: 2. Of those that a mesh axis runs over, the one named last changes fastest.
Arguments:
- tokens: bfloat16 [2, 32, 512, 768], P(None, ('replica', 'shard')), may hold values from -6 to 6
- cotangent: bfloat16 [2, 32, 512, 768], P(None, ('replica', 'shard')), may hold values from -6 to 6
- lengths: int32 [64], replicated, may hold values from 128 to 512, as said below
- dealing: int32 [64], replicated, may hold values from 0 to 63, each once
- in_gain: float32 [2, 768], replicated, may hold values from 0.5 to 1.5
- w_in: bfloat16 [2, 768, 3352], P(None, 'shard'), may hold values from -0.21875 to 0.21875
- conv_w: float32 [2, 4, 1792], replicated, may hold values from -3 to 3
- conv_b: float32 [2, 1792], replicated, may hold values from -3 to 3
- dt_bias: float32 [2, 24], replicated, may hold values from -6.9 to -2.3
- a_log: float32 [2, 24], replicated, may hold values from 0 to 2.77
- d_skip: float32 [2, 24], replicated, may hold values from 0.1 to 1.9
- out_gain: float32 [2, 1536], replicated, may hold values from 0.5 to 1.5
- w_out: bfloat16 [2, 1536, 768], P(None, 'shard'), may hold values from -0.15625 to 0.15625
Outputs:
- outputs: bfloat16 [2, 32, 512, 768], P(None, ('replica', 'shard'))
- grad_tokens: float32 [2, 32, 512, 768], P(None, ('replica', 'shard'))
- grad_in_gain: float32 [2, 768], replicated
- grad_w_in: float32 [2, 768, 3352], P(None, 'shard')
- grad_conv_w: float32 [2, 4, 1792], replicated
- grad_conv_b: float32 [2, 1792], replicated
- grad_dt_bias: float32 [2, 24], replicated
- grad_a_log: float32 [2, 24], replicated
- grad_d_skip: float32 [2, 24], replicated
- grad_out_gain: float32 [2, 1536], replicated
- grad_w_out: float32 [2, 1536, 768], P(None, 'shard')
Inputs may be any that keep to these rules, and one draw needn't show every extreme that they name: `lengths`: one sequence has exactly 512 tokens; the others at least a quarter of that.
All inputs are finite; a program needn't handle non-finite values.
Results may differ from a plain program's by a relative error of at most 0.011.
Values may be sent and summed in bfloat16 or wider, within the bound.
A program may use at most 208 MiB of HBM per device.

v0:
```python
import jax
import jax.numpy as jnp
from jax import lax
from jax.experimental import pallas as pl
from jax.experimental.pallas import tpu as pltpu
from jax.sharding import PartitionSpec as P

D = 768
DI = 1536
NH = 24
HEAD = 64
NSTATE = 128
KW = 4
CONV_CH = 1792
NIN = 3352
LAYERS = 2
MICRO = 2
CH = 128
PAIRS = NH // 2
LANE = 128
DUP = 32
LOG2E = 1.4426950408889634
SUMS = 2048
CUT = 1664
GATHER_BOTH = ((0, 3, 7, 8), (0, 5, 8, 8), (0, 7, 8, 8))
GATHER_LAST = ((1, 4, 6, 8),)
REDUCE_OUT = ((1, 2, 3, 4, 5, 6, 7, 8),)
REDUCE_BOTH = ((0, 1, 2, 3, 4, 5, 6, 7), (0, 1, 2, 4, 5, 6, 7, 8), (0, 3, 5, 7, 8))

epsilon = 1e-05
f32 = jnp.float32
bf16 = jnp.bfloat16
MESH = pl.DeviceIdType.MESH


def mm(a, b):
    return jnp.dot(a, b, preferred_element_type=f32)


def mm_t(a, b):
    return lax.dot_general(a, b, (((1,), (1,)), ((), ())), preferred_element_type=f32)


def t_mm(a, b):
    return lax.dot_general(a, b, (((0,), (0,)), ((), ())), preferred_element_type=f32)


def sigmoid(v):
    return 0.5 * jnp.tanh(0.5 * v) + 0.5


def softplus(v):
    return jnp.maximum(v, 0.0) + jnp.log1p(jnp.exp(-jnp.abs(v)))


def lanes(j, base=0):
    return slice(base + LANE * j, base + LANE * (j + 1))


def norm_scale(stream):
    return lax.rsqrt(jnp.mean(stream * stream, axis=-1, keepdims=True) + epsilon)


def split_pair(v):
    left = lax.broadcasted_iota(jnp.int32, v.shape, 1) < HEAD
    zero = jnp.zeros_like(v)
    return jnp.concatenate([jnp.where(left, v, zero), jnp.where(left, zero, v)], axis=0)


def high_low(v):
    high = v.astype(bf16)
    return high, (v - high.astype(f32)).astype(bf16)


def widen(spread, *values):
    parts = []
    for v in values:
        high, low = high_low(v)
        first = lax.broadcasted_iota(jnp.int32, v.shape, 1) < DUP
        parts.append(jnp.where(first, high, low))
    rows = values[0].shape[0]
    wide = mm(jnp.concatenate(parts, axis=0), spread)
    return [wide[i * rows : (i + 1) * rows] for i in range(len(values))]


def exact_mm(mask, v):
    high, low = high_low(v)
    rest = (v - high.astype(f32) - low.astype(f32)).astype(bf16)
    out = mm(mask.astype(f32).astype(bf16), jnp.concatenate([high, low, rest], axis=1))
    return out[:, :LANE] + out[:, LANE : 2 * LANE] + out[:, 2 * LANE :]


def step_parts(proj_ref, raw_ref, head_ref):
    raw = proj_ref[:, DI + CONV_CH :]
    raw_ref[:, 0:NH] = raw
    raw_ref[:, DUP : DUP + NH] = raw
    shifted = raw_ref[...] + head_ref[0:1]
    step = softplus(shifted)
    rows = lax.broadcasted_iota(jnp.int32, (CH, CH), 0)
    cols = lax.broadcasted_iota(jnp.int32, (CH, CH), 1)
    cum = jnp.dot((cols <= rows).astype(f32), head_ref[1:2] * step, precision=lax.Precision.HIGHEST, preferred_element_type=f32)
    grow = jnp.exp2(cum)
    remain = jnp.exp2(cum[CH - 1 : CH] - cum)
    return shifted, step, cum, cum.T, grow, remain, rows, cols


def conv_block(ext_ref, conv_ref, j):
    total = conv_ref[4:5, lanes(j)]
    for k in range(KW):
        total = total + conv_ref[k : k + 1, lanes(j)] * ext_ref[5 + k : 5 + k + CH, lanes(j)]
    return total


def prepare(layer, params, tables, gather_ref=None):
    in_gain_ref, conv_w_ref, conv_b_ref, dt_bias_ref, a_log_ref, d_skip_ref, out_gain_ref = params
    conv_ref, head_ref, wide_ref, spread_ref = tables
    conv_ref[0:KW] = conv_w_ref[layer]
    conv_ref[KW : KW + 1] = conv_b_ref[layer : layer + 1]
    head_ref[...] = jnp.zeros_like(head_ref)
    rate = -jnp.exp(a_log_ref[layer : layer + 1])
    for row, value in enumerate((dt_bias_ref[layer : layer + 1], rate * LOG2E, rate, d_skip_ref[layer : layer + 1])):
        head_ref[row : row + 1, 0:NH] = value
        head_ref[row : row + 1, DUP : DUP + NH] = value
    column = lax.broadcasted_iota(jnp.int32, (LANE, DI), 0)
    owner = lax.broadcasted_iota(jnp.int32, (LANE, DI), 1) // HEAD
    spread_ref[...] = ((column % DUP == owner) & (column < 2 * DUP)).astype(f32).astype(bf16)
    wide_ref[...] = widen(spread_ref[...], head_ref[...])[0]
    wide_ref[0:1] = wide_ref[3:4]
    wide_ref[1:2] = out_gain_ref[layer : layer + 1]
    if gather_ref is not None:
        column = lax.broadcasted_iota(jnp.int32, (DI, LANE), 1)
        owner = lax.broadcasted_iota(jnp.int32, (DI, LANE), 0) // HEAD
        gather_ref[...] = ((column % DUP == owner) & (column < 2 * DUP)).astype(f32).astype(bf16)


def table_scratch():
    return [
        pltpu.VMEM((8, CONV_CH), f32), pltpu.VMEM((8, LANE), f32), pltpu.VMEM((8, DI), f32), pltpu.VMEM((LANE, DI), bf16),
    ]


def forward_kernel(layer, *refs):
    params, (tokens_ref, w_in_ref), refs = refs[:7], refs[7:9], refs[9:]
    if layer > 0:
        before_ref, w_out_ref, stream_ref, *refs = refs
    normed_ref, proj_ref, mixed_ref, scan_ref, saved_ref, act_ref, slope_ref, *refs = refs
    tables, (ext_ref, raw_ref, state_ref, gated_ref, keep_ref) = refs[:4], refs[4:]
    conv_ref, head_ref, wide_ref, spread_ref = tables

    @pl.when(pl.program_id(1) == 0)
    def _():
        state_ref[...] = jnp.zeros_like(state_ref)
        ext_ref[0:8] = jnp.zeros_like(ext_ref[0:8])

    @pl.when((pl.program_id(0) == 0) & (pl.program_id(1) == 0))
    def _():
        raw_ref[...] = jnp.zeros_like(raw_ref)
        prepare(layer, params, tables)

    stream = tokens_ref[...].astype(f32)
    if layer > 0:
        stream = stream + mm(before_ref[...], w_out_ref[...])
        stream_ref[...] = stream
    normed = stream * norm_scale(stream) * params[0][layer : layer + 1]
    normed_ref[...] = normed.T.astype(bf16)
    proj_ref[...] = mm(normed.astype(bf16), w_in_ref[...])
    ext_ref[8 : 8 + CH] = proj_ref[:, DI : DI + CONV_CH]
    shifted, step, cum, cum_t, grow, remain, rows, cols = step_parts(proj_ref, raw_ref, head_ref)
    step_w, grow_w, remain_w = [widen(spread_ref[...], v)[0] for v in (step, grow, remain * step)]

    def activated(j):
        value = conv_block(ext_ref, conv_ref, j)
        share = sigmoid(value)
        result = value * share
        act_ref[:, lanes(j)] = result
        slope_ref[:, lanes(j)] = share + result * (1.0 - share)
        return result

    b_low = activated(PAIRS).astype(bf16)
    c_low = activated(PAIRS + 1).astype(bf16)
    affinity = jnp.where(cols <= rows, mm_t(c_low, b_low), 0.0)
    state_low = state_ref[...].astype(bf16)
    saved_ref[...] = state_low
    carried = grow_w * mm(c_low, state_low)
    square = jnp.zeros((CH, LANE), f32)
    for j in range(PAIRS):
        xs = activated(j)
        mixing = []
        for h in (2 * j, 2 * j + 1):
            differ = jnp.minimum(cum[:, h : h + 1] - cum_t[h : h + 1], 0.0)
            mixing.append((jnp.exp2(differ) * affinity).astype(bf16))
        keep_ref[:, lanes(j)] = (xs * remain_w[:, lanes(j)]).astype(bf16)
        x_split = split_pair((xs * step_w[:, lanes(j)]).astype(bf16))
        scanned = mm(jnp.concatenate(mixing, axis=1), x_split) + carried[:, lanes(j)]
        scan_ref[:, lanes(j)] = scanned
        gate = proj_ref[:, lanes(j)]
        gated = (scanned + wide_ref[0:1, lanes(j)] * xs) * (gate * sigmoid(gate))
        gated_ref[:, lanes(j)] = gated
        square = square + gated * gated
    state_ref[...] = grow_w[CH - 1 : CH] * state_ref[...] + t_mm(b_low, keep_ref[...])
    scale = lax.rsqrt(jnp.sum(square, axis=1, keepdims=True) * (1.0 / DI) + epsilon)
    mixed_ref[...] = (gated_ref[...] * scale * wide_ref[1:2]).astype(bf16)
    ext_ref[0:8] = ext_ref[CH : CH + 8]


def backward_kernel(layer, *refs):
    params, refs = refs[:7], refs[7:]
    upstream_ref, stream_ref, w_in_ref, w_out_ref, proj_ref, scan_ref, saved_ref, act_ref, slope_ref, *refs = refs
    top = layer == LAYERS - 1
    if top:
        mixed_ref, length_ref, result_ref, *refs = refs
    out_ref, down_ref, sum_ref, *refs = refs
    tables, refs = refs[:4], refs[4:]
    conv_ref, head_ref, wide_ref, spread_ref = tables
    gather_ref, grad_ref, raw_ref, state_ref, gate_ref, dconv_ref, *refs = refs
    keep_ref, grown_ref, terms_ref, row_ref = refs
    chunk = pl.num_programs(1) - 1 - pl.program_id(1)

    @pl.when(pl.program_id(1) == 0)
    def _():
        state_ref[...] = jnp.zeros_like(state_ref)
        dconv_ref[CH : CH + 8] = jnp.zeros_like(dconv_ref[CH : CH + 8])

    @pl.when((pl.program_id(0) == 0) & (pl.program_id(1) == 0))
    def _():
        raw_ref[...] = jnp.zeros_like(raw_ref)
        row_ref[...] = jnp.zeros_like(row_ref)
        sum_ref[...] = jnp.zeros_like(sum_ref)
        prepare(layer, params, tables, gather_ref)

    if top:
        slot = lax.broadcasted_iota(jnp.int32, (CH, D), 0) + chunk * CH
        result = stream_ref[...] + mm(mixed_ref[...], w_out_ref[...])
        result_ref[...] = jnp.where(slot < length_ref[0:1, 0:1], result, 0.0).astype(bf16)
    upstream = upstream_ref[...].astype(f32)
    grad_ref[...] = mm_t(upstream.astype(bf16), w_out_ref[...]).astype(bf16)
    shifted, step, cum, cum_t, grow, remain, rows, cols = step_parts(proj_ref, raw_ref, head_ref)
    step_w, grow_w, remain_w = [widen(spread_ref[...], v)[0] for v in (step, grow, remain)]

    square = jnp.zeros((CH, LANE), f32)
    along = jnp.zeros((CH, LANE), f32)
    for j in range(PAIRS):
        xs = act_ref[:, lanes(j)]
        gate = proj_ref[:, lanes(j)]
        open_share = sigmoid(gate)
        gate_ref[:, lanes(j)] = open_share
        gated = (scan_ref[:, lanes(j)] + wide_ref[0:1, lanes(j)] * xs) * (gate * open_share)
        square = square + gated * gated
        along = along + gated * (grad_ref[:, lanes(j)].astype(f32) * wide_ref[1:2, lanes(j)])
    scale = lax.rsqrt(jnp.sum(square, axis=1, keepdims=True) * (1.0 / DI) + epsilon)
    pull = scale * scale * scale * (jnp.sum(along, axis=1, keepdims=True) * (1.0 / DI))

    b_low = act_ref[:, lanes(PAIRS)].astype(bf16)
    c_low = act_ref[:, lanes(PAIRS + 1)].astype(bf16)
    affinity_t = jnp.where(rows <= cols, mm_t(b_low, c_low), 0.0)
    state = state_ref[...]
    state_low = state.astype(bf16)
    row_ref[1:2] = jnp.sum(saved_ref[...].astype(f32) * state, axis=0, keepdims=True)
    back = remain_w * mm(b_low, state_low)
    affinity_grad = jnp.zeros((CH, CH), f32)
    for j in range(PAIRS):
        xs = act_ref[:, lanes(j)]
        skip = wide_ref[0:1, lanes(j)]
        grad = grad_ref[:, lanes(j)].astype(f32)
        gate = proj_ref[:, lanes(j)]
        open_share = gate_ref[:, lanes(j)]
        opened = gate * open_share
        scanned = scan_ref[:, lanes(j)]
        outer = scanned + skip * xs
        gated = outer * opened
        gated_grad = scale * (grad * wide_ref[1:2, lanes(j)]) - pull * gated
        sum_ref[6:7, lanes(j)] += jnp.sum(grad * (gated * scale), axis=0, keepdims=True)
        dy = gated_grad * opened
        out_ref[:, lanes(j)] = (gated_grad * outer * (open_share + opened * (1.0 - open_share))).astype(bf16)
        sum_ref[5:6, lanes(j)] += jnp.sum(dy * xs, axis=0, keepdims=True)
        dy_low = dy.astype(bf16)
        grown_ref[:, lanes(j)] = (grow_w[:, lanes(j)] * dy).astype(bf16)
        scaled = xs * step_w[:, lanes(j)]
        x_low = scaled.astype(bf16)
        keep_ref[:, lanes(j)] = (scaled * remain_w[:, lanes(j)]).astype(bf16)
        dy_split = split_pair(dy_low)
        kernels = []
        for h in (2 * j, 2 * j + 1):
            differ = jnp.minimum(cum_t[h : h + 1] - cum[:, h : h + 1], 0.0)
            kernels.append(jnp.exp2(differ))
        mixing_t = jnp.concatenate([(k * affinity_t).astype(bf16) for k in kernels], axis=1)
        arrived = back[:, lanes(j)]
        x_grad = mm(mixing_t, dy_split) + arrived
        mixing_grad = mm_t(x_low, dy_split)
        affinity_grad = affinity_grad + mixing_grad[:, :CH] * kernels[0] + mixing_grad[:, CH:] * kernels[1]
        x_back = x_low.astype(f32)
        row_ref[0:1, lanes(j)] = jnp.sum(x_back * arrived, axis=0, keepdims=True)
        high, low = high_low(dy_low.astype(f32) * scanned - x_back * x_grad)
        terms_ref[0:CH, lanes(j)] = high
        terms_ref[CH : 2 * CH, lanes(j)] = low
        terms_ref[2 * CH :, lanes(j)] = (x_grad * xs).astype(bf16)
        dconv_ref[0:CH, lanes(j)] = (step_w[:, lanes(j)] * x_grad + skip * dy) * slope_ref[:, lanes(j)]
    affinity_low = jnp.where(rows <= cols, affinity_grad, 0.0).astype(bf16)
    grown = grown_ref[...]
    b_grad = mm(affinity_low, c_low) + mm_t(keep_ref[...], state_low)
    c_grad = t_mm(affinity_low, b_low) + mm_t(grown, saved_ref[...])
    dconv_ref[0:CH, lanes(PAIRS)] = b_grad * slope_ref[:, lanes(PAIRS)]
    dconv_ref[0:CH, lanes(PAIRS + 1)] = c_grad * slope_ref[:, lanes(PAIRS + 1)]

    gather = gather_ref[...]
    row_sums = mm(jnp.concatenate(high_low(row_ref[...]), axis=0), gather)
    row_sums = row_sums[:8] + row_sums[8:]
    last_grad = row_sums[0:1] + grow[CH - 1 : CH] * row_sums[1:2]
    cum_grad = mm(terms_ref[0:CH], gather) + mm(terms_ref[CH : 2 * CH], gather)
    decay_grad = jnp.dot((cols >= rows).astype(f32), cum_grad, precision=lax.Precision.HIGHEST, preferred_element_type=f32) + last_grad
    step_grad = mm(terms_ref[2 * CH :], gather) + head_ref[2:3] * decay_grad
    raw_grad = step_grad * sigmoid(shifted)
    out_ref[:, DI + CONV_CH :] = raw_grad[:, :NH].astype(bf16)
    sum_ref[7:8, 0:LANE] += jnp.sum(raw_grad, axis=0, keepdims=True)
    sum_ref[7:8, LANE : 2 * LANE] += jnp.sum(decay_grad * step, axis=0, keepdims=True)
    state_ref[...] = grow_w[CH - 1 : CH] * state + t_mm(c_low, grown)

    for j in range(PAIRS + 2):
        taps = [dconv_ref[3 - k : 3 - k + CH, lanes(j)] for k in range(KW)]
        total = conv_ref[0:1, lanes(j)] * taps[0]
        for k in range(1, KW):
            total = total + conv_ref[k : k + 1, lanes(j)] * taps[k]
        out_ref[:, lanes(j, DI)] = total.astype(bf16)
        value = proj_ref[:, lanes(j, DI)]
        for k in range(KW):
            sum_ref[k : k + 1, lanes(j)] += jnp.sum(taps[k] * value, axis=0, keepdims=True)
        sum_ref[4:5, lanes(j)] += jnp.sum(taps[3], axis=0, keepdims=True)
    dconv_ref[CH : CH + 8] = dconv_ref[0:8]

    edge = DI + CONV_CH
    normed_grad = mm_t(out_ref[:, :edge], w_in_ref[:, :edge]) + mm_t(out_ref[:, edge:], w_in_ref[:, edge:])
    stream = stream_ref[...].astype(f32)
    scale = norm_scale(stream)
    sum_ref[7:8, 2 * LANE : 2 * LANE + D] += jnp.sum(normed_grad * (stream * scale), axis=0, keepdims=True)
    inner = normed_grad * params[0][layer : layer + 1]
    pull = scale * scale * scale * jnp.mean(inner * stream, axis=-1, keepdims=True)
    down_ref[...] = upstream_ref[...].astype(f32) + scale * inner - pull * stream


def ring_place(n):
    wide = n // 4
    me = lax.axis_index("shard")
    chip, core = me // 2, me % 2
    row, col = chip // wide, chip % wide
    place = row * (2 * wide - 1 - col) + (1 - row) * col

    def shard_of(at, c):
        at = at % (2 * wide)
        r = at // wide
        x = r * (2 * wide - 1 - at) + (1 - r) * at
        return (r * wide + x) * 2 + c

    return place, core, shard_of


def halves(rows):
    first = rows // 2 // 16 * 16
    return (0, first), (first, rows - first)


def aligned(start, size, unit=16):
    return pl.ds(pl.multiple_of(start, unit), size)


def column_groups(width, replicas, parts):
    unit = LANE * replicas
    units = -(-width // unit)
    parts = min(parts, units)
    groups, start = [], 0
    for g in range(parts):
        size = (units // parts + (g < units % parts)) * unit
        groups.append((start, size, min(size, width - start)))
        start += size
    return groups, start


def remote(src, dst, send, recv, axis, to):
    return pltpu.make_async_remote_copy(
        src_ref=src, dst_ref=dst, send_sem=send, recv_sem=recv, device_id={axis: to}, device_id_type=MESH
    )


def greet(near, across):
    barrier = pltpu.get_barrier_semaphore()
    for to in near:
        pl.semaphore_signal(barrier, inc=1, device_id={"shard": to}, device_id_type=MESH)
    for to in across:
        pl.semaphore_signal(barrier, inc=1, device_id={"replica": to}, device_id_type=MESH)


def meet(count):
    pl.semaphore_wait(pltpu.get_barrier_semaphore(), count)


def bits(count):
    levels = count.bit_length() - 1
    assert 1 << levels == count
    return levels


class Gather:
    def __init__(self, n, arrays, items):
        self.n, self.half = n, n // 4
        self.arrays, self.items = arrays, items
        self.rows = [arrays[i[0]].shape[1] for i in items]

    def in_specs(self):
        return [pl.BlockSpec(memory_space=pl.ANY)] * len(self.arrays)

    out_specs = in_specs

    def out_shapes(self):
        return [jax.ShapeDtypeStruct((a.shape[1] * self.n, a.shape[2]), a.dtype) for a in self.arrays]

    def scratch(self):
        count = len(self.items)
        dma = pltpu.SemaphoreType.DMA
        own = [pltpu.VMEM((rows, i[3]), self.arrays[i[0]].dtype) for rows, i in zip(self.rows, self.items)]
        return [dma((count, self.half, 2, 2)), dma((count, self.half + 1, 2, 2)), dma((count, 2))] + own

    def tracks(self, parts, wholes, scratch):
        ring_sem, pair_sem, own_sem, *own_refs = scratch
        n, half = self.n, self.half
        place, core, shard_of = ring_place(n)
        right, left, pair = shard_of(place + 1, core), shard_of(place + n // 2 - 1, core), shard_of(place, 1 - core)
        me = shard_of(place, core)
        ways = ((0, right), (1, left))

        def rows_of(i, s, d):
            return (0, self.rows[i]) if s < half else halves(self.rows[i])[d]

        def part_at(i, part):
            a, layer, first, wide = self.items[i]
            return parts[a].at[layer, part[0] : part[0] + part[1], first : first + wide]

        def whole_at(i, owner, part):
            a, _, first, wide = self.items[i]
            return wholes[a].at[aligned(owner * self.rows[i] + part[0], part[1]), first : first + wide]

        def hop(i, s, d, to):
            owner = shard_of(place + (n // 2 - (s - 1) if d == 0 else s - 1), core)
            part = rows_of(i, s, d)
            src = part_at(i, part) if s == 1 else whole_at(i, owner, part)
            return remote(src, whole_at(i, owner, part), ring_sem.at[i, s - 1, d, 0], ring_sem.at[i, s - 1, d, 1], "shard", to)

        def cross(i, s, d):
            owner = me if s == 0 else shard_of(place + (n // 2 - s if d == 0 else s), core)
            part = (0, self.rows[i]) if s == 0 else rows_of(i, s, d)
            src = part_at(i, part) if s == 0 else whole_at(i, owner, part)
            return remote(src, whole_at(i, owner, part), pair_sem.at[i, s, d, 0], pair_sem.at[i, s, d, 1], "shard", pair)

        def own_in(i):
            return pltpu.make_async_copy(part_at(i, (0, self.rows[i])), own_refs[i], own_sem.at[i, 0])

        def own_out(i):
            return pltpu.make_async_copy(own_refs[i], whole_at(i, me, (0, self.rows[i])), own_sem.at[i, 1])

        crossings = [(0, 0)] + [(s, d) for s in range(1, half + 1) for d in (0, 1)]

        def start(i):
            for d, to in ways:
                hop(i, 1, d, to).start()
            cross(i, 0, 0).start()
            own_in(i).start()

        def forward(i, s):
            if s == 1:
                own_in(i).wait()
                own_out(i).start()
            for d, to in ways:
                hop(i, s, d, to).wait_recv()
                if s < half:
                    hop(i, s + 1, d, to).start()
                cross(i, s, d).start()

        def last(i):
            for s, d in crossings:
                cross(i, s, d).wait_recv()
            for s, d in crossings:
                cross(i, s, d).wait_send()
            for s in range(1, half + 1):
                for d, to in ways:
                    hop(i, s, d, to).wait_send()
            own_out(i).wait()

        hello = [lambda: greet((right, left, pair), ()), lambda: meet(3)]
        return hello, [
            [lambda i=i: start(i)]
            + [lambda i=i, s=s: forward(i, s) for s in range(1, half + 1)]
            + [lambda i=i: last(i)]
            for i in range(len(self.items))
        ]


class Reduce:
    def __init__(self, n, replicas, shapes, groups, modes=None):
        self.n, self.replicas = n, replicas
        self.chips, self.half, self.levels = n // 2, n // 4, bits(replicas)
        self.shapes = [(r // n, w) for r, w in shapes]
        self.groups = [column_groups(w, replicas, count) for (_, w), count in zip(self.shapes, groups)]
        self.modes = modes or ["full"] * len(shapes)
        self.work = [(a, g) for a in range(len(shapes)) for g in range(len(self.groups[a][0]))]

    def in_specs(self):
        return [pl.BlockSpec(memory_space=pl.ANY)] * len(self.shapes)

    out_specs = in_specs

    def out_shapes(self):
        return [
            jax.ShapeDtypeStruct((rows, padded), bf16) if mode == "head" else jax.ShapeDtypeStruct((rows, width), f32)
            for (rows, width), (_, padded), mode in zip(self.shapes, self.groups, self.modes)
        ]

    each = 12

    def scratch(self):
        dma = pltpu.SemaphoreType.DMA
        items = []
        for (rows, width), (groups, padded), mode in zip(self.shapes, self.groups, self.modes):
            g = len(groups)
            plane = (rows, width) if mode != "tail" else (16, LANE)
            far = (rows, padded) if mode != "head" else (16, LANE)
            items += [
                pltpu.VMEM((self.chips,) + plane, bf16),
                pltpu.VMEM((self.chips,) + plane, bf16),
                pltpu.VMEM((self.half, 2) + plane, bf16),
                pltpu.VMEM((self.half, 2) + plane, bf16),
                pltpu.VMEM((rows, padded), bf16),
                pltpu.VMEM((self.levels,) + far, bf16),
                pltpu.VMEM(far, bf16),
                pltpu.VMEM((rows, width) if mode != "head" else (16, LANE), f32),
                dma((g, self.chips, 3)), dma((g, self.half, 2, 2)), dma((g, 2 * self.levels, 2)), dma((g,)),
            ]
        return items

    def tracks(self, ins, outs, scratch, feed=None):
        n, replicas, chips, half, levels = self.n, self.replicas, self.chips, self.half, self.levels
        place, core, shard_of = ring_place(n)
        right, left, pair = shard_of(place + 1, core), shard_of(place + chips - 1, core), shard_of(place, 1 - core)
        mine = lax.axis_index("replica")
        ways = ((0, right), (1, left))
        order = [half] + [v for s in range(half - 1, 0, -1) for v in (s, chips - s)] + [0]
        buffers = [scratch[self.each * a : self.each * (a + 1)] for a in range(len(self.shapes))]

        def partner(j):
            bit = mine // (1 << j) % 2
            return mine + (1 - 2 * bit) * (1 << j), bit

        def cols_of(a, g):
            start, _, wide = self.groups[a][0][g]
            return slice(start, start + wide)

        def piece(a, g, owner):
            rows = self.shapes[a][0]
            return ins[a].at[aligned(owner * rows, rows), cols_of(a, g)]

        def pairing(a, g, q):
            sem = buffers[a][8]
            return remote(piece(a, g, shard_of(place + q, 1 - core)), buffers[a][1].at[q, :, cols_of(a, g)], sem.at[g, q, 0], sem.at[g, q, 1], "shard", pair)

        def loading(a, g, q):
            return pltpu.make_async_copy(
                piece(a, g, shard_of(place + q, core)), buffers[a][0].at[q, :, cols_of(a, g)], buffers[a][8].at[g, q, 2]
            )

        def part_of(a, k, d):
            rows = self.shapes[a][0]
            return halves(rows)[d] if k == 1 else (0, rows)

        def ringing(a, g, k, d, to):
            first, count = part_of(a, k, d)
            sem = buffers[a][9]
            return remote(
                buffers[a][2].at[k - 1, d, first : first + count, cols_of(a, g)],
                buffers[a][3].at[k - 1, d, first : first + count, cols_of(a, g)],
                sem.at[g, k - 1, d, 0], sem.at[g, k - 1, d, 1], "shard", to,
            )

        def region(a, g, j, keep):
            start, size, _ = self.groups[a][0][g]
            at = start
            for i in range(j + 1):
                bit = mine // (1 << i) % 2
                at = at + (bit if keep or i < j else 1 - bit) * (size >> (i + 1))
            return aligned(at, size >> (j + 1), LANE)

        def halving(a, g, j):
            cols = region(a, g, j, False)
            sem = buffers[a][10]
            return remote(
                buffers[a][4].at[:, cols], buffers[a][5].at[j, :, cols], sem.at[g, j, 0], sem.at[g, j, 1], "replica", partner(j)[0]
            )

        def doubling(a, g, j):
            cols = region(a, g, j, True)
            sem = buffers[a][10]
            return remote(
                buffers[a][6].at[:, cols], buffers[a][6].at[:, cols],
                sem.at[g, levels + j, 0], sem.at[g, levels + j, 1], "replica", partner(j)[0],
            )

        def storing(a, g):
            cols = cols_of(a, g)
            return pltpu.make_async_copy(buffers[a][7].at[:, cols], outs[a].at[:, cols], buffers[a][11].at[g])

        def both(a, g, q, part):
            first, count = part
            rows, cols = slice(first, first + count), cols_of(a, g)
            return buffers[a][0][q, rows, cols].astype(f32) + buffers[a][1][q, rows, cols].astype(f32)

        def arrived(a, g, q):
            if not (feed and a == 0):
                loading(a, g, q).wait()
            pairing(a, g, q).wait_recv()

        def begin(a, g):
            fed = feed and a == 0
            if fed:
                feed(g, cols_of(a, g))
            for q in order:
                pairing(a, g, q).start()
                if fed:
                    buffers[a][0][q, :, cols_of(a, g)] = piece(a, g, shard_of(place + q, core))[...]
                else:
                    loading(a, g, q).start()

        def turn(a, g, k):
            cols = cols_of(a, g)
            for d, to in ways:
                q = half - k + 1 if d == 0 else chips - (half - k + 1)
                if k > 1 or d == 0:
                    arrived(a, g, q)
                if k > 1:
                    ringing(a, g, k - 1, d, to).wait_recv()
                pieces = [part_of(a, 1, d)] if k == 1 else halves(self.shapes[a][0]) if k == 2 else [part_of(a, k, d)]
                for e, (at, many) in enumerate(pieces):
                    value = both(a, g, q, (at, many))
                    if k > 2 or (k == 2 and e == d):
                        value = value + buffers[a][3][k - 2, d, at : at + many, cols].astype(f32)
                    buffers[a][2][k - 1, d, at : at + many, cols] = value.astype(bf16)
                ringing(a, g, k, d, to).start()

        def settle(a, g):
            cols = cols_of(a, g)
            start, size, wide = self.groups[a][0][g]
            rows = self.shapes[a][0]
            arrived(a, g, 0)
            value = both(a, g, 0, (0, rows))
            for d, to in ways:
                ringing(a, g, half, d, to).wait_recv()
                value = value + buffers[a][3][half - 1, d, :, cols].astype(f32)
            buffers[a][4][:, cols] = value.astype(bf16)
            if wide < size:
                buffers[a][4][:, start + wide : start + size] = jnp.zeros((rows, size - wide), bf16)
            if self.modes[a] == "head":
                handing(a, g).start()
            else:
                halving(a, g, 0).start()

        def handing(a, g):
            start, size, _ = self.groups[a][0][g]
            cols = slice(start, start + size)
            here, there = buffers[a][4].at[:, cols], (outs if self.modes[a] == "head" else ins)[a].at[:, cols]
            if self.modes[a] == "tail":
                here, there = there, here
            return pltpu.make_async_copy(here, there, buffers[a][11].at[g])

        def resume(a, g):
            handing(a, g).wait()
            halving(a, g, 0).start()

        def halve(a, g, j):
            halving(a, g, j).wait_recv()
            cols = region(a, g, j, True)
            value = (buffers[a][4][:, cols].astype(f32) + buffers[a][5][j, :, cols].astype(f32)).astype(bf16)
            if j + 1 < levels:
                buffers[a][4][:, cols] = value
                halving(a, g, j + 1).start()
            else:
                buffers[a][6][:, cols] = value
                doubling(a, g, j).start()

        def double(a, g, j):
            doubling(a, g, j).wait_recv()
            if j > 0:
                doubling(a, g, j - 1).start()

        def last(a, g):
            double(a, g, 0)
            cols = cols_of(a, g)
            buffers[a][7][:, cols] = buffers[a][6][:, cols].astype(f32)
            storing(a, g).start()
            if self.modes[a] != "tail":
                leave(a, g)
            for j in range(levels):
                halving(a, g, j).wait_send()
                doubling(a, g, j).wait_send()
            storing(a, g).wait()

        def leave(a, g):
            for q in order:
                pairing(a, g, q).wait_send()
            for k in range(1, half + 1):
                for d, to in ways:
                    ringing(a, g, k, d, to).wait_send()

        def part(a, g):
            leave(a, g)
            handing(a, g).wait()

        across = [partner(j)[0] for j in range(levels)]
        hello = [lambda: greet((right, left, pair), across), lambda: meet(3 + levels)]
        def track(a, g):
            planes = (
                [lambda: begin(a, g)]
                + [lambda k=k: turn(a, g, k) for k in range(1, half + 1)]
                + [lambda: settle(a, g)]
            )
            rest = (
                [lambda j=j: halve(a, g, j) for j in range(levels)]
                + [lambda j=j: double(a, g, j) for j in range(levels - 1, 0, -1)]
                + [lambda: last(a, g)]
            )
            if self.modes[a] == "head":
                return planes + [lambda: part(a, g)]
            if self.modes[a] == "tail":
                return [lambda: handing(a, g).start(), lambda: resume(a, g)] + rest
            return planes + rest

        return hello, [track(a, g) for a, g in self.work]


def beside(body, counts, engine, times, hooks):
    ins, outs, scratch = counts

    def kernel(*refs):
        i = len(engine.in_specs())
        o = len(engine.out_specs())
        own_in, refs = refs[:ins], refs[ins:]
        far_in, refs = refs[:i], refs[i:]
        own_out, refs = refs[:outs], refs[outs:]
        far_out, refs = refs[:o], refs[o:]
        own_scratch, far_scratch = refs[:scratch], refs[scratch:]
        hello, tracks = engine.tracks(far_in, far_out, far_scratch)
        plan = {}
        plan[0] = [hello[0]]
        plan.setdefault(min(t[0] for t in times), []).append(hello[1])
        for t, track in enumerate(tracks):
            wanted = times[t]
            if len(wanted) != len(track):
                first = wanted[0]
                wanted = [first + (hooks - first) * i // (len(track) - 1) for i in range(len(track))]
            for at, stage in zip(wanted, track):
                plan.setdefault(min(at, hooks), []).append(stage)
        step = pl.program_id(0) * pl.num_programs(1) + pl.program_id(1)

        def run(at):
            for stage in plan[at]:
                stage()

        pl.when(step == 0)(lambda: run(0))
        body(*own_in, *own_out, *own_scratch)
        for at in sorted(plan):
            if at > 0:
                pl.when(step == at - 1)(lambda at=at: run(at))

    return kernel


def move(engine, operands, collective_id, name):
    def kernel(*refs):
        i, o = len(engine.in_specs()), len(engine.out_specs())
        hello, tracks = engine.tracks(refs[:i], refs[i : i + o], refs[i + o :])
        for stage in hello:
            stage()
        for at in range(max(map(len, tracks))):
            for track in tracks:
                if at < len(track):
                    track[at]()

    return pl.pallas_call(
        kernel,
        out_shape=engine.out_shapes(),
        in_specs=engine.in_specs(),
        out_specs=engine.out_specs(),
        scratch_shapes=engine.scratch(),
        compiler_params=pltpu.CompilerParams(collective_id=collective_id, has_side_effects=True),
        name=name,
    )(*operands)


def finish_kernel(engine, n, replicas, *refs):
    left_ref, right_hbm, first_ref, second_ref, in_ref, out0_ref, out1_ref = refs[:7]
    in_total_ref, out_total_ref, total_ref = refs[7:10]
    product_ref, right_ref, mine_ref, plane_ref, across_ref, whole_ref, in_buf, out_buf = refs[10:18]
    plane_sem, across_sem, share_sem, copy_sem, right_sem, *scratch = refs[18:]
    me, mine = lax.axis_index("shard"), lax.axis_index("replica")
    width = mine_ref.shape[2]

    def operand(g):
        start, _, wide = engine.groups[0][0][g]
        cols = slice(start, start + wide)
        return pltpu.make_async_copy(right_hbm.at[:, cols], right_ref.at[:, cols], right_sem.at[g])

    for g in range(len(engine.groups[0][0])):
        operand(g).start()

    ready = set()

    def feed(g, cols):
        if g in ready:
            return
        ready.add(g)
        operand(g).wait()
        product_ref[:, cols] = mm(left_ref[...], right_ref[:, cols]).astype(bf16)

    _, tracks = engine.tracks((product_ref, out0_ref), (in_total_ref.at[0], out_total_ref.at[0]), scratch, feed)
    greet([(me + s) % n for s in range(1, n)], [(mine + s) % replicas for s in range(1, replicas)])
    moves = [(in_ref, in_buf, in_total_ref.at[1]), (out1_ref, out_buf, out_total_ref.at[1])]
    fetches = [pltpu.make_async_copy(src, via, copy_sem.at[0, i]) for i, (src, via, _) in enumerate(moves)]
    stores = [pltpu.make_async_copy(via, dst, copy_sem.at[1, i]) for i, (_, via, dst) in enumerate(moves)]
    for fetch in fetches:
        fetch.start()
    spots = [(k // (n // 2), k % (n // 2) * width) for k in range(n)]
    for k, (half, at) in enumerate(spots):
        mine_ref[k] = (second_ref if half else first_ref)[:, at : at + width]

    def plane(s):
        to = (me + s) % n
        return remote(mine_ref.at[to], plane_ref.at[s], plane_sem.at[0, s], plane_sem.at[1, s], "shard", to)

    def across(s):
        return remote(across_ref.at[0], across_ref.at[s], across_sem.at[0, s], across_sem.at[1, s], "replica", (mine + s) % replicas)

    def share(s):
        return remote(whole_ref.at[me], whole_ref.at[me], share_sem.at[0, s], share_sem.at[1, s], "shard", (me + s) % n)

    def sharing(s):
        owner = (me + n - s) % n
        return remote(whole_ref.at[owner], whole_ref.at[owner], share_sem.at[0, s], share_sem.at[1, s], "shard", (me + s) % n)

    def send_small():
        for s in range(1, n):
            plane(s).start()

    def sum_plane():
        value = mine_ref[me]
        for s in range(1, n):
            plane(s).wait_recv()
            value = value + plane_ref[s]
        across_ref[0] = value
        for s in range(1, replicas):
            across(s).start()

    def sum_across():
        for s in range(1, replicas):
            across(s).wait_recv()
        zero = jnp.zeros((8, width), f32)
        whole_ref[me] = lax.fori_loop(0, replicas, lambda i, acc: acc + across_ref[(mine - i + replicas) % replicas], zero)
        for s in range(1, n):
            share(s).start()

    def give_small():
        for s in range(1, n):
            sharing(s).wait_recv()
        for k, (half, at) in enumerate(spots):
            total_ref[8 * half : 8 * half + 8, at : at + width] = whole_ref[k]

    plan = {}
    for (a, g), track in zip(engine.work, tracks):
        for i, stage in enumerate(track):
            plan.setdefault(((g if a == 0 else 0) + (2 * i - 1 if i else 0), i), []).append(stage)
    feed(0, slice(0, engine.groups[0][0][0][2]))
    meet(n + replicas - 2)
    slots = sorted(plan)
    for k, slot in enumerate(slots):
        for stage in plan[slot]:
            stage()
        if k == 0:
            send_small()
        if k == len(slots) // 4:
            sum_plane()
            for fetch, store in zip(fetches, stores):
                fetch.wait()
                store.start()
        if k == len(slots) // 2:
            sum_across()
    give_small()
    for s in range(1, n):
        plane(s).wait_send()
        share(s).wait_send()
    for s in range(1, replicas):
        across(s).wait_send()
    for store in stores:
        store.wait()


def finish(left, right, sums, in_grad, out_grads, n, replicas, collective_id):
    rows, width = left.shape[0] // n, right.shape[1]
    out_rows, out_width = out_grads[1].shape
    engine = Reduce(n, replicas, [(left.shape[0], width), (out_rows * n, out_width)], [7, 1], ["full", "tail"])
    anywhere, vmem = pl.BlockSpec(memory_space=pl.ANY), pl.BlockSpec(memory_space=pltpu.VMEM)
    dma = pltpu.SemaphoreType.DMA
    small = (8, 2 * SUMS // n)
    return pl.pallas_call(
        lambda *refs: finish_kernel(engine, n, replicas, *refs),
        out_shape=[
            jax.ShapeDtypeStruct((LAYERS, rows, width), f32),
            jax.ShapeDtypeStruct((LAYERS, out_rows, out_width), f32),
            jax.ShapeDtypeStruct((LAYERS * 8, SUMS), f32),
        ],
        in_specs=[vmem, anywhere, vmem, vmem] + [anywhere] * 3,
        out_specs=[anywhere, anywhere, vmem],
        scratch_shapes=[
            pltpu.VMEM((n * rows, width), bf16),
            pltpu.VMEM(right.shape, bf16),
            pltpu.VMEM((n,) + small, f32),
            pltpu.VMEM((n,) + small, f32),
            pltpu.VMEM((replicas,) + small, f32),
            pltpu.VMEM((n,) + small, f32),
            pltpu.VMEM((rows, width), f32),
            pltpu.VMEM((out_rows, out_width), f32),
            dma((2, n)), dma((2, replicas)), dma((2, n)), dma((2, 2)), dma((len(engine.groups[0][0]),)),
        ] + engine.scratch(),
        compiler_params=pltpu.CompilerParams(collective_id=collective_id, has_side_effects=True, vmem_limit_bytes=60 * 2**20),
        name="finish",
    )(left, right, *sums, in_grad, *out_grads)


def small_kernel(total_ref, a_log_ref, gain_ref, conv_w_ref, conv_b_ref, dt_bias_ref, a_log_grad_ref, d_skip_ref, out_gain_ref):
    column = lax.broadcasted_iota(jnp.int32, (DI, LANE), 1)
    owner = lax.broadcasted_iota(jnp.int32, (DI, LANE), 0) // HEAD
    gather = (column == owner).astype(f32).astype(bf16)
    for l in range(LAYERS):
        here, row = slice(l, l + 1), 8 * l
        gain_ref[here] = total_ref[row + 7 : row + 8, 2 * LANE : 2 * LANE + D]
        conv_w_ref[l] = total_ref[row : row + KW, :CONV_CH]
        conv_b_ref[here] = total_ref[row + 4 : row + 5, :CONV_CH]
        dt_bias_ref[here] = total_ref[row + 7 : row + 8, 0:NH]
        a_log_grad_ref[here] = -jnp.exp(a_log_ref[here]) * total_ref[row + 7 : row + 8, LANE : LANE + NH]
        out_gain_ref[here] = total_ref[row + 6 : row + 7, :DI]
        value = total_ref[row : row + 8, :DI]
        high = value.astype(bf16)
        middle = (value - high.astype(f32)).astype(bf16)
        low = (value - high.astype(f32) - middle.astype(f32)).astype(bf16)
        summed = mm(high, gather) + mm(middle, gather) + mm(low, gather)
        d_skip_ref[here] = summed[5:6, 0:NH]


def small_results(total, params):
    return pl.pallas_call(
        small_kernel,
        out_shape=[jax.ShapeDtypeStruct(p.shape, f32) for p in params],
        name="small_results",
    )(total, params[4])


def product_kernel(left_ref, right_ref, out_ref):
    out_ref[...] = mm(left_ref[...], right_ref[...]).astype(bf16)


def product(left, right, wide):
    (rows, depth), width = left.shape, right.shape[1]
    return pl.pallas_call(
        product_kernel,
        grid=(pl.cdiv(width, wide),),
        in_specs=[pl.BlockSpec((rows, depth), lambda c: (0, 0)), pl.BlockSpec((depth, wide), lambda c: (0, c))],
        out_specs=pl.BlockSpec((rows, wide), lambda c: (0, c)),
        out_shape=jax.ShapeDtypeStruct((rows, width), bf16),
        compiler_params=pltpu.CompilerParams(vmem_limit_bytes=62 * 2**20),
        name="product",
    )(left, right)


def turned_kernel(left_ref, right_ref, out_ref):
    out_ref[...] = t_mm(left_ref[...], right_ref[...].astype(bf16)).astype(bf16)


def turned_product(left, right, tall):
    (depth, rows), width = left.shape, right.shape[1]
    return pl.pallas_call(
        turned_kernel,
        grid=(rows // tall,),
        in_specs=[pl.BlockSpec((depth, tall), lambda r: (0, r)), pl.BlockSpec((depth, width), lambda r: (0, 0))],
        out_specs=pl.BlockSpec((tall, width), lambda r: (r, 0)),
        out_shape=jax.ShapeDtypeStruct((rows, width), bf16),
        compiler_params=pltpu.CompilerParams(vmem_limit_bytes=62 * 2**20),
        name="turned_product",
    )(left, right)


def top_kernel(row_total, slots, left_ref, cotangent_ref, lengths_ref, dealing_ref, out_ref, upstream_ref, length_ref):
    @pl.when(pl.program_id(0) == 0)
    def _():
        mine = lax.axis_index("replica") * lax.axis_size("shard") + lax.axis_index("shard")
        place = lax.broadcasted_iota(jnp.int32, lengths_ref.shape, 1)
        dealing, lengths = dealing_ref[...].astype(f32), lengths_ref[...].astype(f32)
        slot = lax.broadcasted_iota(jnp.int32, (slots, D), 0)
        for m in range(MICRO):
            sequence = jnp.sum(jnp.where(place == m * row_total + mine, dealing, 0.0), axis=1, keepdims=True)
            length = jnp.sum(jnp.where(place.astype(f32) == sequence, lengths, 0.0), axis=1, keepdims=True).astype(jnp.int32)
            length_ref[8 * m : 8 * m + 8] = jnp.broadcast_to(length, (8, LANE))
            here = slice(m * slots, (m + 1) * slots)
            upstream_ref[here] = jnp.where(slot < length, cotangent_ref[here].astype(f32), 0.0).astype(bf16)

    out_ref[...] = t_mm(left_ref[...], upstream_ref[...]).astype(bf16)


def top_product(left, cotangent, lengths, dealing, row_total, tall):
    (depth, rows), width = left.shape, cotangent.shape[1]
    whole = lambda shape: pl.BlockSpec(shape, lambda r: (0, 0))
    sequences = lengths.shape[0]
    return pl.pallas_call(
        lambda *refs: top_kernel(row_total, depth // MICRO, *refs),
        grid=(rows // tall,),
        in_specs=[pl.BlockSpec((depth, tall), lambda r: (0, r)), whole((depth, width)), whole((1, sequences)), whole((1, sequences))],
        out_specs=[pl.BlockSpec((tall, width), lambda r: (r, 0)), whole((depth, width)), whole((8 * MICRO, LANE))],
        out_shape=[
            jax.ShapeDtypeStruct((rows, width), bf16),
            jax.ShapeDtypeStruct((depth, width), bf16),
            jax.ShapeDtypeStruct((8 * MICRO, LANE), jnp.int32),
        ],
        compiler_params=pltpu.CompilerParams(vmem_limit_bytes=62 * 2**20),
        name="top_product",
    )(left, cotangent, lengths.reshape(1, sequences), dealing.reshape(1, sequences))


def fixed(shape):
    return pl.BlockSpec(shape, lambda r, c: (0,) * len(shape))


def held(shape):
    return pl.BlockSpec(shape, lambda r, c: (0,) * len(shape), pipeline_mode=pl.Buffered(1))


def grid_call(body, grid, operands, in_specs, out_specs, out_shapes, scratch, name, extra):
    engine, given, times, collective_id = extra
    kernel = beside(body, (len(in_specs), len(out_specs), len(scratch)), engine, times, grid[0] * grid[1])
    return pl.pallas_call(
        kernel, grid=grid, in_specs=in_specs + engine.in_specs(), out_specs=out_specs + engine.out_specs(),
        out_shape=out_shapes + engine.out_shapes(), scratch_shapes=scratch + engine.scratch(),
        compiler_params=pltpu.CompilerParams(
            dimension_semantics=("arbitrary", "arbitrary"), vmem_limit_bytes=60 * 2**20,
            collective_id=collective_id, has_side_effects=True,
        ),
        name=name,
    )(*operands, *given)


def layer_forward(layer, tokens, w_in, before, w_out, params, chunks, extra):
    count = tokens.shape[0]
    block = lambda r, c: (r * chunks + c, 0)
    later = layer > 0
    rows = lambda width: pl.BlockSpec((CH, width), block)
    return grid_call(
        lambda *refs: forward_kernel(layer, *refs),
        (count // (chunks * CH), chunks),
        (*params, tokens, w_in) + ((before, w_out) if later else ()),
        [held(p.shape) for p in params] + [rows(D), held((D, NIN))] + ([rows(DI), held((DI, D))] if later else []),
        ([rows(D)] if later else [])
        + [pl.BlockSpec((D, CH), lambda r, c: (0, r * chunks + c)), rows(NIN), rows(DI), rows(DI), pl.BlockSpec((NSTATE, DI), block), rows(CONV_CH), rows(CONV_CH)],
        ([jax.ShapeDtypeStruct((count, D), f32)] if later else [])
        + [
            jax.ShapeDtypeStruct((D, count), bf16),
            jax.ShapeDtypeStruct((count, NIN), f32),
            jax.ShapeDtypeStruct((count, DI), bf16),
            jax.ShapeDtypeStruct((count, DI), f32),
            jax.ShapeDtypeStruct((count // CH * NSTATE, DI), bf16),
            jax.ShapeDtypeStruct((count, CONV_CH), f32),
            jax.ShapeDtypeStruct((count, CONV_CH), f32),
        ],
        table_scratch()
        + [
            pltpu.VMEM((CH + 8, CONV_CH), f32),
            pltpu.VMEM((CH, LANE), f32),
            pltpu.VMEM((NSTATE, DI), f32),
            pltpu.VMEM((CH, DI), f32),
            pltpu.VMEM((CH, DI), bf16),
        ],
        f"layer_forward_{layer}", extra,
    )


def layer_backward(layer, upstream, stream, w_in, w_out, projected, kept, mixed, length, params, chunks, extra):
    count = projected.shape[0]
    block = lambda r, c: (r * chunks + chunks - 1 - c, 0)
    rows = lambda width: pl.BlockSpec((CH, width), block)
    top = layer == LAYERS - 1
    return grid_call(
        lambda *refs: backward_kernel(layer, *refs),
        (count // (chunks * CH), chunks),
        (*params, upstream, stream, w_in, w_out, projected, *kept) + ((mixed, length) if top else ()),
        [held(p.shape) for p in params]
        + [rows(D), rows(D), held((D, NIN)), held((DI, D)), rows(NIN), rows(DI), pl.BlockSpec((NSTATE, DI), block), rows(CONV_CH), rows(CONV_CH)]
        + ([rows(DI), pl.BlockSpec((8, LANE), lambda r, c: (r, 0))] if top else []),
        ([rows(D)] if top else []) + [rows(NIN), rows(D), fixed((8, SUMS))],
        ([jax.ShapeDtypeStruct((count, D), bf16)] if top else [])
        + [
            jax.ShapeDtypeStruct((count, NIN), bf16),
            jax.ShapeDtypeStruct((count, D), f32),
            jax.ShapeDtypeStruct((8, SUMS), f32),
        ],
        table_scratch()
        + [
            pltpu.VMEM((DI, LANE), bf16),
            pltpu.VMEM((CH, DI), bf16),
            pltpu.VMEM((CH, LANE), f32),
            pltpu.VMEM((NSTATE, DI), f32),
            pltpu.VMEM((CH, DI), f32),
            pltpu.VMEM((CH + 8, CONV_CH), f32),
            pltpu.VMEM((CH, DI), bf16),
            pltpu.VMEM((CH, DI), bf16),
            pltpu.VMEM((3 * CH, DI), bf16),
            pltpu.VMEM((8, DI), f32),
        ],
        f"layer_backward_{layer}", extra,
    )


def shards(
    tokens, cotangent, lengths, dealing, in_gain, w_in, conv_w, conv_b, dt_bias, a_log, d_skip, out_gain, w_out,
):
    n, replicas = lax.axis_size("shard"), lax.axis_size("replica")
    slot_count = tokens.shape[2]
    chunks = slot_count // CH
    count = MICRO * slot_count
    params = (in_gain, conv_w, conv_b, dt_bias, a_log, d_skip, out_gain)
    flat = tokens.reshape(count, D)

    (first_in,) = move(Gather(n, [w_in], [(0, 0, 0, CUT), (0, 0, CUT, NIN - CUT)]), (w_in,), 1, "gather_first")
    engine = Gather(n, [w_out, w_in], [(0, 0, 0, D), (1, 1, 0, CUT), (1, 1, CUT, NIN - CUT)])
    normed0, projected0, mixed0, *kept0, first_out, second_in = layer_forward(
        0, flat, first_in, None, None, params, chunks, (engine, (w_out, w_in), GATHER_BOTH, 2)
    )
    engine = Gather(n, [w_out], [(0, 1, 0, D)])
    stream, normed1, projected1, mixed1, *kept1, second_out = layer_forward(
        1, flat, second_in, mixed0, first_out, params, chunks, (engine, (w_out,), GATHER_LAST, 3)
    )

    out_grad1, upstream, length = top_product(mixed1, cotangent.reshape(count, D), lengths, dealing, replicas * n, 512)
    engine = Reduce(n, replicas, [out_grad1.shape], [1])
    result, project_grad1, upstream1, sums1, out_total1 = layer_backward(
        1, upstream, stream, second_in, second_out, projected1, kept1, mixed1, length, params, chunks,
        (engine, (out_grad1,), REDUCE_OUT, 4),
    )
    in_grad1 = product(normed1, project_grad1, 512)
    out_grad0 = turned_product(mixed0, upstream1, 512)
    engine = Reduce(n, replicas, [in_grad1.shape, out_grad0.shape], [2, 1], ["full", "head"])
    project_grad0, upstream0, sums0, in_total1, out_total0 = layer_backward(
        0, upstream1, flat, first_in, first_out, projected0, kept0, None, None, params, chunks,
        (engine, (in_grad1, out_grad0), REDUCE_BOTH, 5),
    )
    in_total, out_total, small = finish(
        normed0, project_grad0, (sums0, sums1), in_total1, (out_total0, out_total1), n, replicas, 6
    )
    gain_grad, *small = small_results(small, params)
    shape = (MICRO, 1, slot_count, D)
    return (result.reshape(shape), upstream0.reshape(shape), gain_grad, in_total, *small, out_total)


def solution(mesh):
    rows = P(None, ("replica", "shard"), None, None)
    split = P(None, "shard", None)
    in_specs = (rows, rows, P(), P(), P(), split, P(), P(), P(), P(), P(), P(), split)
    out_specs = (rows, rows, P(), split, P(), P(), P(), P(), P(), P(), split)
    return jax.shard_map(shards, mesh=mesh, in_specs=in_specs, out_specs=out_specs, check_vma=False)
```

profile of v0, /device:TPU:0, one launch (start us, length us, event | category | flops | bytes accessed | tf_op | source)
XLA Modules:
  0.0 343.2 jit_solution(5018431188220618978)
XLA Ops:
  0.6 28.6 %gather_first.1.refs_8_.refs_9_ = bf16[768,3352]{1,0:T(8,128)(2,1)} custom-call(bf16[2,96,3352]{2,1,0:T(8,128)(2,1)} %refs_10_.1), custom_call_target="tpu_custom_call" | custom-call | tf_op jit(solution)/shard_map/gather_first/pallas_call | solution.py:782
  29.2 41.5 %layer_forward_0.1 = (bf16[768,1024]{1,0:T(8,128)(2,1)}, f32[1024,3352]{1,0:T(8,128)}, bf16[1024,1536]{1,0:T(8,128)(2,1)}, f32[1024,1536]{1,0:T(8,128)}, bf16[10...) custom-call(f32[2,768]{1,0:T(2,128)} %refs_0_.9, ...), custom_call_target="tpu_custom_call" | custom-call | tf_op jit(solution)/shard_map/layer_forward_0/pallas_call | solution.py:1040
  70.8 39.7 %layer_forward_1.1 = (f32[1024,768]{1,0:T(8,128)}, bf16[768,1024]{1,0:T(8,128)(2,1)}, f32[1024,3352]{1,0:T(8,128)}, bf16[1024,1536]{1,0:T(8,128)(2,1)}, f32[1024...) custom-call(f32[2,768]{1,0:T(2,128)} %refs_0_.9, ...), custom_call_target="tpu_custom_call" | custom-call | tf_op jit(solution)/shard_map/layer_forward_1/pallas_call | solution.py:1040
  110.5 6.9 %top_product.1 = (bf16[1536,768]{1,0:T(8,128)(2,1)}, bf16[1024,768]{1,0:T(8,128)(2,1)}, s32[16,128]{1,0:T(8,128)}) custom-call(bf16[1024,1536]{1,0:T(8,128)(2,1)} %get-tuple-element.55.refs_0_.refs_16_, bf16[1024,768]{1,0:T(8,128)(2,1)} %bitcast.14, s32[1,64]{1,0:T(1,128)} %bitcast.16, s32[1,64]{1,0:T(1,128)} %bitcast.17), custom_call_target="tpu_custom_call" | custom-call | tf_op jit(solution)/shard_map/top_product/pallas_call | solution.py:1014
  117.4 69.4 %layer_backward_1.1 = (bf16[1024,768]{1,0:T(8,128)(2,1)}, bf16[1024,3352]{1,0:T(8,128)(2,1)}, f32[1024,768]{1,0:T(8,128)}, f32[8,2048]{1,0:T(8,128)}, f32[192,768]{1,0:T(8,128)}) custom-call(f32[2,768]{1,0:T(2,128)} %refs_0_.9, f32[2,4,1792]{2,1,0:T(4,128)} %refs_1_.7, f32[2,1792]{1,0:T(2,128)} %refs_2_.7, f32[2,24]{1,0:T(2,128)} %refs_3_.7, ...), custom_call_target="tpu_custom_call" | custom-call | tf_op jit(solution)/shard_map/layer_backward_1/pallas_call | solution.py:1040
  186.8 6.7 %turned_product.1.refs_17_ = bf16[1536,768]{1,0:T(8,128)(2,1)} custom-call(bf16[1024,1536]{1,0:T(8,128)(2,1)} %get-tuple-element.53.refs_9_.left_ref, f32[1024,768]{1,0:T(8,128)} %get-tuple-element.67.right_ref.refs_7_), custom_call_target="tpu_custom_call" | custom-call | tf_op jit(solution)/shard_map/turned_product/pallas_call | solution.py:982
  193.5 11.1 %product.1.refs_16_ = bf16[768,3352]{1,0:T(8,128)(2,1)} custom-call(bf16[768,1024]{1,0:T(8,128)(2,1)} %get-tuple-element.73.left_ref, bf16[1024,3352]{1,0:T(8,128)(2,1)} %get-tuple-element.74.right_ref), custom_call_target="tpu_custom_call" | custom-call | tf_op jit(solution)/shard_map/product/pallas_call | solution.py:965
  204.6 75.4 %layer_backward_0.1 = (bf16[1024,3352]{1,0:T(8,128)(2,1)}, f32[1024,768]{1,0:T(8,128)}, f32[8,2048]{1,0:T(8,128)}, f32[96,3352]{1,0:T(8,128)}, bf16[192,1024]{1,0:T(8,128)(2,1)}) custom-call(f32[2,768]{1,0:T(2,128)} %refs_0_.9, f32[2,4,1792]{2,1,0:T(4,128)} %refs_1_.7, f32[2,1792]{1,0:T(2,128)} %refs_2_.7, f32[2,24]{1,0:T(2,128)} %refs_3_.7, ...), custom_call_target="tpu_custom_call" | custom-call | tf_op jit(solution)/shard_map/layer_backward_0/pallas_call | solution.py:1040
  280.0 52.4 %finish.1 = (f32[2,96,3352]{2,1,0:T(8,128)}, f32[2,192,768]{2,1,0:T(8,128)}, f32[16,2048]{1,0:T(8,128)}) custom-call(bf16[768,1024]{1,0:T(8,128)(2,1)} %get-tuple-element.76.refs_0_, bf16[1024,3352]{1,0:T(8,128)(2,1)} %get-tuple-element.77.refs_1_, f32[8,2048]{1,0:T(8,128)} %get-tuple-element.78.refs_2_, f32[8,2048]{1,0:T(8,128)} %get-tuple-element.79.refs_3_, ...), custom_call_target="tpu_custom_call" | custom-call | tf_op jit(solution)/shard_map/finish/pallas_call | solution.py:906
  332.4 0.0 copy-start
  332.4 2.1 small_results.1
  334.6 2.7 copy.30
  337.2 0.0 copy-done
  337.2 0.0 copy-start.1
  337.2 1.7 copy.31
  338.9 1.2 copy-done.1
  340.1 0.0 copy-start.2
  340.1 1.5 copy.32
  341.6 0.6 copy-done.2
  342.2 1.0 copy.33
Async XLA Ops:
  332.4 4.8 %copy-start = (f32[1024,768]{1,0:T(8,128)S(1)}, f32[1024,768]{1,0:T(8,128)}, u32[]{:S(2)}) copy-start(f32[1024,768]{1,0:T(8,128)} %get-tuple-element.75) | copy-start | bytes 9437188
  337.2 2.9 copy-start.1
  340.1 2.1 copy-start.2
where the time goes:
time: 344 us; the launch traced here: 343 us
  Pallas kernels  334 us (97%)
  local copies, waits for them, and re-layouts  8.65 us (3%)
    pallas_call x4, Pallas kernels, grid_call(): pl.pallas_call(kernel, grid=grid, in_specs=in_specs + engine.in_specs(),...  226 us
    pallas_call x1, Pallas kernels, finish(): pl.pallas_call(lambda *refs: finish_kernel(engine, n, replicas, *refs), o...  52.4 us
    pallas_call x1, Pallas kernels, move(): pl.pallas_call(kernel, out_shape=engine.out_shapes(), in_specs=engine.in_...  28.6 us
    pallas_call x1, Pallas kernels, product(): pl.pallas_call(product_kernel, grid=(pl.cdiv(width, wide),), in_specs=[pl...  11.1 us
    unnamed x10, local copies, waits for them, and re-layouts  8.65 us
    pallas_call x1, Pallas kernels, top_product(): pl.pallas_call(lambda *refs: top_kernel(row_total, depth // MICRO, *refs)...  6.9 us

commit v1 on v0

--- a/solution.py
+++ b/solution.py
@@ -213,7 +213,7 @@
     tables, refs = refs[:4], refs[4:]
     conv_ref, head_ref, wide_ref, spread_ref = tables
     gather_ref, grad_ref, raw_ref, state_ref, gate_ref, dconv_ref, *refs = refs
-    keep_ref, grown_ref, terms_ref, row_ref = refs
+    keep_ref, grown_ref, terms_ref, row_ref, back_ref = refs
     chunk = pl.num_programs(1) - 1 - pl.program_id(1)
 
     @pl.when(pl.program_id(1) == 0)
@@ -228,10 +228,6 @@
         sum_ref[...] = jnp.zeros_like(sum_ref)
         prepare(layer, params, tables, gather_ref)
 
-    if top:
-        slot = lax.broadcasted_iota(jnp.int32, (CH, D), 0) + chunk * CH
-        result = stream_ref[...] + mm(mixed_ref[...], w_out_ref[...])
-        result_ref[...] = jnp.where(slot < length_ref[0:1, 0:1], result, 0.0).astype(bf16)
     upstream = upstream_ref[...].astype(f32)
     grad_ref[...] = mm_t(upstream.astype(bf16), w_out_ref[...]).astype(bf16)
     shifted, step, cum, cum_t, grow, remain, rows, cols = step_parts(proj_ref, raw_ref, head_ref)
@@ -258,6 +254,11 @@
     row_ref[1:2] = jnp.sum(saved_ref[...].astype(f32) * state, axis=0, keepdims=True)
     back = remain_w * mm(b_low, state_low)
     affinity_grad = jnp.zeros((CH, CH), f32)
+
+    def back_from(first, end):
+        part = mm_t(out_ref[:, first:end], w_in_ref[:, first:end])
+        back_ref[...] = part if first == 0 else back_ref[...] + part
+
     for j in range(PAIRS):
         xs = act_ref[:, lanes(j)]
         skip = wide_ref[0:1, lanes(j)]
@@ -295,6 +296,8 @@
         terms_ref[CH : 2 * CH, lanes(j)] = low
         terms_ref[2 * CH :, lanes(j)] = (x_grad * xs).astype(bf16)
         dconv_ref[0:CH, lanes(j)] = (step_w[:, lanes(j)] * x_grad + skip * dy) * slope_ref[:, lanes(j)]
+        if j % 4 == 3:
+            back_from(LANE * (j - 3), LANE * (j + 1))
     affinity_low = jnp.where(rows <= cols, affinity_grad, 0.0).astype(bf16)
     grown = grown_ref[...]
     b_grad = mm(affinity_low, c_low) + mm_t(keep_ref[...], state_low)
@@ -325,10 +328,17 @@
         for k in range(KW):
             sum_ref[k : k + 1, lanes(j)] += jnp.sum(taps[k] * value, axis=0, keepdims=True)
         sum_ref[4:5, lanes(j)] += jnp.sum(taps[3], axis=0, keepdims=True)
+        if top and j == 1:
+            slot = lax.broadcasted_iota(jnp.int32, (CH, D), 0) + chunk * CH
+            result = stream_ref[...] + mm(mixed_ref[...], w_out_ref[...])
+            result_ref[...] = jnp.where(slot < length_ref[0:1, 0:1], result, 0.0).astype(bf16)
+        if j in (3, 7, 11):
+            back_from(DI + LANE * (j - 3), DI + LANE * (j + 1))
     dconv_ref[CH : CH + 8] = dconv_ref[0:8]
 
-    edge = DI + CONV_CH
-    normed_grad = mm_t(out_ref[:, :edge], w_in_ref[:, :edge]) + mm_t(out_ref[:, edge:], w_in_ref[:, edge:])
+    back_from(2 * DI, DI + CONV_CH)
+    back_from(DI + CONV_CH, NIN)
+    normed_grad = back_ref[...]
     stream = stream_ref[...].astype(f32)
     scale = norm_scale(stream)
     sum_ref[7:8, 2 * LANE : 2 * LANE + D] += jnp.sum(normed_grad * (stream * scale), axis=0, keepdims=True)
@@ -928,7 +938,18 @@
     )(left, right, *sums, in_grad, *out_grads)
 
 
-def small_kernel(total_ref, a_log_ref, gain_ref, conv_w_ref, conv_b_ref, dt_bias_ref, a_log_grad_ref, d_skip_ref, out_gain_ref):
+def results_kernel(count, total_ref, a_log_ref, *refs):
+    from_refs, refs = refs[:count], refs[count:]
+    to_refs, refs = refs[:count], refs[count:]
+    gain_ref, conv_w_ref, conv_b_ref, dt_bias_ref, a_log_grad_ref, d_skip_ref, out_gain_ref, *refs = refs
+    via_refs, sem = refs[:count], refs[count]
+    fetches = [pltpu.make_async_copy(a, b, sem.at[0, i]) for i, (a, b) in enumerate(zip(from_refs, via_refs))]
+    stores = [pltpu.make_async_copy(a, b, sem.at[1, i]) for i, (a, b) in enumerate(zip(via_refs, to_refs))]
+    for fetch in fetches:
+        fetch.start()
+    for fetch, store in zip(fetches, stores):
+        fetch.wait()
+        store.start()
     column = lax.broadcasted_iota(jnp.int32, (DI, LANE), 1)
     owner = lax.broadcasted_iota(jnp.int32, (DI, LANE), 0) // HEAD
     gather = (column == owner).astype(f32).astype(bf16)
@@ -946,31 +967,53 @@
         low = (value - high.astype(f32) - middle.astype(f32)).astype(bf16)
         summed = mm(high, gather) + mm(middle, gather) + mm(low, gather)
         d_skip_ref[here] = summed[5:6, 0:NH]
-
-
-def small_results(total, params):
-    return pl.pallas_call(
-        small_kernel,
-        out_shape=[jax.ShapeDtypeStruct(p.shape, f32) for p in params],
-        name="small_results",
-    )(total, params[4])
-
-
-def product_kernel(left_ref, right_ref, out_ref):
+    for store in stores:
+        store.wait()
+
+
+def results(total, params, moved):
+    anywhere, vmem = pl.BlockSpec(memory_space=pl.ANY), pl.BlockSpec(memory_space=pltpu.VMEM)
+    count = len(moved)
+    out = pl.pallas_call(
+        lambda *refs: results_kernel(count, *refs),
+        in_specs=[vmem, vmem] + [anywhere] * count,
+        out_specs=[anywhere] * count + [vmem] * len(params),
+        out_shape=[jax.ShapeDtypeStruct(m.shape, m.dtype) for m in moved] + [jax.ShapeDtypeStruct(p.shape, f32) for p in params],
+        scratch_shapes=[pltpu.VMEM(m.shape, m.dtype) for m in moved] + [pltpu.SemaphoreType.DMA((2, count))],
+        compiler_params=pltpu.CompilerParams(vmem_limit_bytes=62 * 2**20),
+        name="results",
+    )(total, params[4], *moved)
+    return out[:count], out[count:]
+
+
+def product_kernel(left_ref, right_ref, from_ref, out_ref, to_ref, via_ref, sem):
+    step, last = pl.program_id(0), pl.num_programs(0) - 1
+    fetch = pltpu.make_async_copy(from_ref, via_ref, sem.at[0])
+    store = pltpu.make_async_copy(via_ref, to_ref, sem.at[1])
+    pl.when(step == 0)(fetch.start)
     out_ref[...] = mm(left_ref[...], right_ref[...]).astype(bf16)
 
-
-def product(left, right, wide):
+    @pl.when(step == 1)
+    def _():
+        fetch.wait()
+        store.start()
+
+    pl.when(step == last)(store.wait)
+
+
+def product(left, right, wide, moved):
     (rows, depth), width = left.shape, right.shape[1]
+    anywhere = pl.BlockSpec(memory_space=pl.ANY)
     return pl.pallas_call(
         product_kernel,
         grid=(pl.cdiv(width, wide),),
-        in_specs=[pl.BlockSpec((rows, depth), lambda c: (0, 0)), pl.BlockSpec((depth, wide), lambda c: (0, c))],
-        out_specs=pl.BlockSpec((rows, wide), lambda c: (0, c)),
-        out_shape=jax.ShapeDtypeStruct((rows, width), bf16),
+        in_specs=[pl.BlockSpec((rows, depth), lambda c: (0, 0)), pl.BlockSpec((depth, wide), lambda c: (0, c)), anywhere],
+        out_specs=[pl.BlockSpec((rows, wide), lambda c: (0, c)), anywhere],
+        out_shape=[jax.ShapeDtypeStruct((rows, width), bf16), jax.ShapeDtypeStruct(moved.shape, moved.dtype)],
+        scratch_shapes=[pltpu.VMEM(moved.shape, moved.dtype), pltpu.SemaphoreType.DMA((2,))],
         compiler_params=pltpu.CompilerParams(vmem_limit_bytes=62 * 2**20),
         name="product",
-    )(left, right)
+    )(left, right, moved)
 
 
 def turned_kernel(left_ref, right_ref, out_ref):
@@ -1113,6 +1156,7 @@
             pltpu.VMEM((CH, DI), bf16),
             pltpu.VMEM((3 * CH, DI), bf16),
             pltpu.VMEM((8, DI), f32),
+            pltpu.VMEM((CH, D), f32),
         ],
         f"layer_backward_{layer}", extra,
     )
@@ -1144,7 +1188,7 @@
         1, upstream, stream, second_in, second_out, projected1, kept1, mixed1, length, params, chunks,
         (engine, (out_grad1,), REDUCE_OUT, 4),
     )
-    in_grad1 = product(normed1, project_grad1, 512)
+    in_grad1, result = product(normed1, project_grad1, 512, result)
     out_grad0 = turned_product(mixed0, upstream1, 512)
     engine = Reduce(n, replicas, [in_grad1.shape, out_grad0.shape], [2, 1], ["full", "head"])
     project_grad0, upstream0, sums0, in_total1, out_total0 = layer_backward(
@@ -1154,7 +1198,7 @@
     in_total, out_total, small = finish(
         normed0, project_grad0, (sums0, sums1), in_total1, (out_total0, out_total1), n, replicas, 6
     )
-    gain_grad, *small = small_results(small, params)
+    (upstream0, in_total, out_total), (gain_grad, *small) = results(small, params, (upstream0, in_total, out_total))
     shape = (MICRO, 1, slot_count, D)
     return (result.reshape(shape), upstream0.reshape(shape), gain_grad, in_total, *small, out_total)
 

time: 344 us -> 333 us (0.968)
  local copies, waits for them, and re-layouts: 8.65 us -> 0 us
    unnamed x10 -> x0, local copies, waits for them, and re-layouts: 8.65 us -> none
    pallas_call x4, Pallas kernels: 226 us -> 219 us  [grid_call(): pl.pallas_call(kernel, grid=grid, in_specs=in_specs + engine.in_specs(),...]
    pallas_call x1, Pallas kernels: 2.15 us -> 6.41 us  [results(): pl.pallas_call(lambda *refs: results_kernel(count, *refs), in_specs=[vmem...]
where the time goes in v1:
time: 333 us; the launch traced here: 332 us
  Pallas kernels  331 us (99%)
    pallas_call x4, Pallas kernels, grid_call(): pl.pallas_call(kernel, grid=grid, in_specs=in_specs + engine.in_specs(),...  219 us
    pallas_call x1, Pallas kernels, finish(): pl.pallas_call(lambda *refs: finish_kernel(engine, n, replicas, *refs), o...  52.3 us
    pallas_call x1, Pallas kernels, move(): pl.pallas_call(kernel, out_shape=engine.out_shapes(), in_specs=engine.in_...  28.6 us
    pallas_call x1, Pallas kernels, product(): pl.pallas_call(product_kernel, grid=(pl.cdiv(width, wide),), in_specs=[pl...  11.3 us
    pallas_call x1, Pallas kernels, top_product(): pl.pallas_call(lambda *refs: top_kernel(row_total, depth // MICRO, *refs)...  6.9 us
    pallas_call x1, Pallas kernels, turned_product(): pl.pallas_call(turned_kernel, grid=(rows // tall,), in_specs=[pl.BlockSpe...  6.7 us

profile of v1, /device:TPU:0, one launch (start us, length us, event | category | flops | bytes accessed | tf_op | source)
XLA Modules:
  0.0 332.1 jit_solution(1385163184006365352)
XLA Ops:
  0.6 28.6 %gather_first.1.refs_8_.refs_9_ = bf16[768,3352]{1,0:T(8,128)(2,1)} custom-call(bf16[2,96,3352]{2,1,0:T(8,128)(2,1)} %refs_10_.1), custom_call_target="tpu_custom_call" | custom-call | tf_op jit(solution)/shard_map/gather_first/pallas_call | solution.py:792
  29.2 41.5 %layer_forward_0.1 = (bf16[768,1024]{1,0:T(8,128)(2,1)}, f32[1024,3352]{1,0:T(8,128)}, bf16[1024,1536]{1,0:T(8,128)(2,1)}, f32[1024,1536]{1,0:T(8,128)}, bf16[10...) custom-call(f32[2,768]{1,0:T(2,128)} %refs_0_.9, ...), custom_call_target="tpu_custom_call" | custom-call | tf_op jit(solution)/shard_map/layer_forward_0/pallas_call | solution.py:1083
  70.8 39.7 %layer_forward_1.1 = (f32[1024,768]{1,0:T(8,128)}, bf16[768,1024]{1,0:T(8,128)(2,1)}, f32[1024,3352]{1,0:T(8,128)}, bf16[1024,1536]{1,0:T(8,128)(2,1)}, f32[1024...) custom-call(f32[2,768]{1,0:T(2,128)} %refs_0_.9, ...), custom_call_target="tpu_custom_call" | custom-call | tf_op jit(solution)/shard_map/layer_forward_1/pallas_call | solution.py:1083
  110.5 6.9 %top_product.1 = (bf16[1536,768]{1,0:T(8,128)(2,1)}, bf16[1024,768]{1,0:T(8,128)(2,1)}, s32[16,128]{1,0:T(8,128)}) custom-call(bf16[1024,1536]{1,0:T(8,128)(2,1)} %get-tuple-element.61.refs_0_.refs_16_, bf16[1024,768]{1,0:T(8,128)(2,1)} %bitcast.13, s32[1,64]{1,0:T(1,128)} %bitcast.14, s32[1,64]{1,0:T(1,128)} %bitcast.15), custom_call_target="tpu_custom_call" | custom-call | tf_op jit(solution)/shard_map/top_product/pallas_call | solution.py:1057
  117.4 65.5 %layer_backward_1.1 = (bf16[1024,768]{1,0:T(8,128)(2,1)}, bf16[1024,3352]{1,0:T(8,128)(2,1)}, f32[1024,768]{1,0:T(8,128)}, f32[8,2048]{1,0:T(8,128)}, f32[192,768]{1,0:T(8,128)}) custom-call(f32[2,768]{1,0:T(2,128)} %refs_0_.9, f32[2,4,1792]{2,1,0:T(4,128)} %refs_1_.8, f32[2,1792]{1,0:T(2,128)} %refs_2_.7, f32[2,24]{1,0:T(2,128)} %refs_3_.7, ...), custom_call_target="tpu_custom_call" | custom-call | tf_op jit(solution)/shard_map/layer_backward_1/pallas_call | solution.py:1083
  182.9 6.7 %turned_product.1.refs_17_ = bf16[1536,768]{1,0:T(8,128)(2,1)} custom-call(bf16[1024,1536]{1,0:T(8,128)(2,1)} %get-tuple-element.58.refs_9_.left_ref, f32[1024,768]{1,0:T(8,128)} %get-tuple-element.76.right_ref.refs_7_), custom_call_target="tpu_custom_call" | custom-call | tf_op jit(solution)/shard_map/turned_product/pallas_call | solution.py:1025
  189.6 11.3 %product.1 = (bf16[768,3352]{1,0:T(8,128)(2,1)}, bf16[1024,768]{1,0:T(8,128)(2,1)}) custom-call(bf16[768,1024]{1,0:T(8,128)(2,1)} %get-tuple-element.60.left_ref, bf16[1024,3352]{1,0:T(8,128)(2,1)} %get-tuple-element.72.right_ref, bf16[1024,768]{1,0:T(8,128)(2,1)} %get-tuple-element.73.from_ref), custom_call_target="tpu_custom_call" | custom-call | tf_op jit(solution)/shard_map/product/pallas_call | solution.py:1007
  200.9 72.3 %layer_backward_0.1 = (bf16[1024,3352]{1,0:T(8,128)(2,1)}, f32[1024,768]{1,0:T(8,128)}, f32[8,2048]{1,0:T(8,128)}, f32[96,3352]{1,0:T(8,128)}, bf16[192,1024]{1,0:T(8,128)(2,1)}) custom-call(f32[2,768]{1,0:T(2,128)} %refs_0_.9, f32[2,4,1792]{2,1,0:T(4,128)} %refs_1_.8, f32[2,1792]{1,0:T(2,128)} %refs_2_.7, f32[2,24]{1,0:T(2,128)} %refs_3_.7, ...), custom_call_target="tpu_custom_call" | custom-call | tf_op jit(solution)/shard_map/layer_backward_0/pallas_call | solution.py:1083
  273.2 52.3 %finish.1 = (f32[2,96,3352]{2,1,0:T(8,128)}, f32[2,192,768]{2,1,0:T(8,128)}, f32[16,2048]{1,0:T(8,128)}) custom-call(bf16[768,1024]{1,0:T(8,128)(2,1)} %get-tuple-element.75.refs_0_, bf16[1024,3352]{1,0:T(8,128)(2,1)} %get-tuple-element.83.refs_1_, f32[8,2048]{1,0:T(8,128)} %get-tuple-element.84.refs_2_, f32[8,2048]{1,0:T(8,128)} %get-tuple-element.85.refs_3_, ...), custom_call_target="tpu_custom_call" | custom-call | tf_op jit(solution)/shard_map/finish/pallas_call | solution.py:916
  325.5 6.4 %results.1 = (f32[1024,768]{1,0:T(8,128)}, f32[2,96,3352]{2,1,0:T(8,128)}, f32[2,192,768]{2,1,0:T(8,128)}, f32[2,768]{1,0:T(2,128)}, f32[2,4,1792]{2,1,0:T(4,128...) custom-call(f32[16,2048]{1,0:T(8,128)} %get-tuple-element.89.refs_0_, ...), custom_call_target="tpu_custom_call" | custom-call | tf_op jit(solution)/shard_map/results/pallas_call | solution.py:977

commit v2 on v1

--- a/solution.py
+++ b/solution.py
@@ -298,26 +298,6 @@
         dconv_ref[0:CH, lanes(j)] = (step_w[:, lanes(j)] * x_grad + skip * dy) * slope_ref[:, lanes(j)]
         if j % 4 == 3:
             back_from(LANE * (j - 3), LANE * (j + 1))
-    affinity_low = jnp.where(rows <= cols, affinity_grad, 0.0).astype(bf16)
-    grown = grown_ref[...]
-    b_grad = mm(affinity_low, c_low) + mm_t(keep_ref[...], state_low)
-    c_grad = t_mm(affinity_low, b_low) + mm_t(grown, saved_ref[...])
-    dconv_ref[0:CH, lanes(PAIRS)] = b_grad * slope_ref[:, lanes(PAIRS)]
-    dconv_ref[0:CH, lanes(PAIRS + 1)] = c_grad * slope_ref[:, lanes(PAIRS + 1)]
-
-    gather = gather_ref[...]
-    row_sums = mm(jnp.concatenate(high_low(row_ref[...]), axis=0), gather)
-    row_sums = row_sums[:8] + row_sums[8:]
-    last_grad = row_sums[0:1] + grow[CH - 1 : CH] * row_sums[1:2]
-    cum_grad = mm(terms_ref[0:CH], gather) + mm(terms_ref[CH : 2 * CH], gather)
-    decay_grad = jnp.dot((cols >= rows).astype(f32), cum_grad, precision=lax.Precision.HIGHEST, preferred_element_type=f32) + last_grad
-    step_grad = mm(terms_ref[2 * CH :], gather) + head_ref[2:3] * decay_grad
-    raw_grad = step_grad * sigmoid(shifted)
-    out_ref[:, DI + CONV_CH :] = raw_grad[:, :NH].astype(bf16)
-    sum_ref[7:8, 0:LANE] += jnp.sum(raw_grad, axis=0, keepdims=True)
-    sum_ref[7:8, LANE : 2 * LANE] += jnp.sum(decay_grad * step, axis=0, keepdims=True)
-    state_ref[...] = grow_w[CH - 1 : CH] * state + t_mm(c_low, grown)
-
     for j in range(PAIRS + 2):
         taps = [dconv_ref[3 - k : 3 - k + CH, lanes(j)] for k in range(KW)]
         total = conv_ref[0:1, lanes(j)] * taps[0]
@@ -328,6 +308,27 @@
         for k in range(KW):
             sum_ref[k : k + 1, lanes(j)] += jnp.sum(taps[k] * value, axis=0, keepdims=True)
         sum_ref[4:5, lanes(j)] += jnp.sum(taps[3], axis=0, keepdims=True)
+        if j == 3:
+            affinity_low = jnp.where(rows <= cols, affinity_grad, 0.0).astype(bf16)
+            grown = grown_ref[...]
+            b_grad = mm(affinity_low, c_low) + mm_t(keep_ref[...], state_low)
+            c_grad = t_mm(affinity_low, b_low) + mm_t(grown, saved_ref[...])
+            dconv_ref[0:CH, lanes(PAIRS)] = b_grad * slope_ref[:, lanes(PAIRS)]
+            dconv_ref[0:CH, lanes(PAIRS + 1)] = c_grad * slope_ref[:, lanes(PAIRS + 1)]
+        if j == 8:
+            gather = gather_ref[...]
+            row_sums = mm(jnp.concatenate(high_low(row_ref[...]), axis=0), gather)
+            row_sums = row_sums[:8] + row_sums[8:]
+            last_grad = row_sums[0:1] + grow[CH - 1 : CH] * row_sums[1:2]
+            cum_grad = mm(terms_ref[0:CH], gather) + mm(terms_ref[CH : 2 * CH], gather)
+            decay_grad = jnp.dot((cols >= rows).astype(f32), cum_grad, precision=lax.Precision.HIGHEST, preferred_element_type=f32) + last_grad
+            step_grad = mm(terms_ref[2 * CH :], gather) + head_ref[2:3] * decay_grad
+            raw_grad = step_grad * sigmoid(shifted)
+            out_ref[:, DI + CONV_CH :] = raw_grad[:, :NH].astype(bf16)
+            sum_ref[7:8, 0:LANE] += jnp.sum(raw_grad, axis=0, keepdims=True)
+            sum_ref[7:8, LANE : 2 * LANE] += jnp.sum(decay_grad * step, axis=0, keepdims=True)
+        if j == 5:
+            state_ref[...] = grow_w[CH - 1 : CH] * state + t_mm(c_low, grown)
         if top and j == 1:
             slot = lax.broadcasted_iota(jnp.int32, (CH, D), 0) + chunk * CH
             result = stream_ref[...] + mm(mixed_ref[...], w_out_ref[...])
@@ -1188,8 +1189,8 @@
         1, upstream, stream, second_in, second_out, projected1, kept1, mixed1, length, params, chunks,
         (engine, (out_grad1,), REDUCE_OUT, 4),
     )
-    in_grad1, result = product(normed1, project_grad1, 512, result)
-    out_grad0 = turned_product(mixed0, upstream1, 512)
+    in_grad1, result = product(normed1, project_grad1, 1024, result)
+    out_grad0 = turned_product(mixed0, upstream1, 768)
     engine = Reduce(n, replicas, [in_grad1.shape, out_grad0.shape], [2, 1], ["full", "head"])
     project_grad0, upstream0, sums0, in_total1, out_total0 = layer_backward(
         0, upstream1, flat, first_in, first_out, projected0, kept0, None, None, params, chunks,

time: 333 us -> 327 us (0.982)
  Pallas kernels: 331 us -> 326 us
    pallas_call x4, Pallas kernels: 219 us -> 215 us  [grid_call(): pl.pallas_call(kernel, grid=grid, in_specs=in_specs + engine.in_specs(),...]
where the time goes in v2:
time: 327 us; the launch traced here: 326 us
  Pallas kernels  326 us (100%)
    pallas_call x4, Pallas kernels, grid_call(): pl.pallas_call(kernel, grid=grid, in_specs=in_specs + engine.in_specs(),...  215 us
    pallas_call x1, Pallas kernels, finish(): pl.pallas_call(lambda *refs: finish_kernel(engine, n, replicas, *refs), o...  52.4 us
    pallas_call x1, Pallas kernels, move(): pl.pallas_call(kernel, out_shape=engine.out_shapes(), in_specs=engine.in_...  28.6 us
    pallas_call x1, Pallas kernels, product(): pl.pallas_call(product_kernel, grid=(pl.cdiv(width, wide),), in_specs=[pl...  10.5 us
    pallas_call x1, Pallas kernels, top_product(): pl.pallas_call(lambda *refs: top_kernel(row_total, depth // MICRO, *refs)...  6.9 us

profile of v2, /device:TPU:0, one launch (start us, length us, event | category | flops | bytes accessed | tf_op | source)
XLA Modules:
  0.0 326.5 jit_solution(10290408550331072415)
XLA Ops:
  0.6 28.6 %gather_first.1.refs_8_.refs_9_ = bf16[768,3352]{1,0:T(8,128)(2,1)} custom-call(bf16[2,96,3352]{2,1,0:T(8,128)(2,1)} %refs_10_.1), custom_call_target="tpu_custom_call" | custom-call | tf_op jit(solution)/shard_map/gather_first/pallas_call | solution.py:793
  29.2 41.5 %layer_forward_0.1 = (bf16[768,1024]{1,0:T(8,128)(2,1)}, f32[1024,3352]{1,0:T(8,128)}, bf16[1024,1536]{1,0:T(8,128)(2,1)}, f32[1024,1536]{1,0:T(8,128)}, bf16[10...) custom-call(f32[2,768]{1,0:T(2,128)} %refs_0_.9, ...), custom_call_target="tpu_custom_call" | custom-call | tf_op jit(solution)/shard_map/layer_forward_0/pallas_call | solution.py:1084
  70.8 39.7 %layer_forward_1.1 = (f32[1024,768]{1,0:T(8,128)}, bf16[768,1024]{1,0:T(8,128)(2,1)}, f32[1024,3352]{1,0:T(8,128)}, bf16[1024,1536]{1,0:T(8,128)(2,1)}, f32[1024...) custom-call(f32[2,768]{1,0:T(2,128)} %refs_0_.9, ...), custom_call_target="tpu_custom_call" | custom-call | tf_op jit(solution)/shard_map/layer_forward_1/pallas_call | solution.py:1084
  110.5 6.9 %top_product.1 = (bf16[1536,768]{1,0:T(8,128)(2,1)}, bf16[1024,768]{1,0:T(8,128)(2,1)}, s32[16,128]{1,0:T(8,128)}) custom-call(bf16[1024,1536]{1,0:T(8,128)(2,1)} %get-tuple-element.61.refs_0_.refs_16_, bf16[1024,768]{1,0:T(8,128)(2,1)} %bitcast.13, s32[1,64]{1,0:T(1,128)} %bitcast.14, s32[1,64]{1,0:T(1,128)} %bitcast.15), custom_call_target="tpu_custom_call" | custom-call | tf_op jit(solution)/shard_map/top_product/pallas_call | solution.py:1058
  117.4 62.9 %layer_backward_1.1 = (bf16[1024,768]{1,0:T(8,128)(2,1)}, bf16[1024,3352]{1,0:T(8,128)(2,1)}, f32[1024,768]{1,0:T(8,128)}, f32[8,2048]{1,0:T(8,128)}, f32[192,768]{1,0:T(8,128)}) custom-call(f32[2,768]{1,0:T(2,128)} %refs_0_.9, f32[2,4,1792]{2,1,0:T(4,128)} %refs_1_.8, f32[2,1792]{1,0:T(2,128)} %refs_2_.7, f32[2,24]{1,0:T(2,128)} %refs_3_.7, ...), custom_call_target="tpu_custom_call" | custom-call | tf_op jit(solution)/shard_map/layer_backward_1/pallas_call | solution.py:1084
  180.3 6.3 %turned_product.1.refs_17_ = bf16[1536,768]{1,0:T(8,128)(2,1)} custom-call(bf16[1024,1536]{1,0:T(8,128)(2,1)} %get-tuple-element.58.refs_9_.left_ref, f32[1024,768]{1,0:T(8,128)} %get-tuple-element.76.right_ref.refs_7_), custom_call_target="tpu_custom_call" | custom-call | tf_op jit(solution)/shard_map/turned_product/pallas_call | solution.py:1026
  186.6 10.5 %product.1 = (bf16[768,3352]{1,0:T(8,128)(2,1)}, bf16[1024,768]{1,0:T(8,128)(2,1)}) custom-call(bf16[768,1024]{1,0:T(8,128)(2,1)} %get-tuple-element.60.left_ref, bf16[1024,3352]{1,0:T(8,128)(2,1)} %get-tuple-element.72.right_ref, bf16[1024,768]{1,0:T(8,128)(2,1)} %get-tuple-element.73.from_ref), custom_call_target="tpu_custom_call" | custom-call | tf_op jit(solution)/shard_map/product/pallas_call | solution.py:1008
  197.1 70.3 %layer_backward_0.1 = (bf16[1024,3352]{1,0:T(8,128)(2,1)}, f32[1024,768]{1,0:T(8,128)}, f32[8,2048]{1,0:T(8,128)}, f32[96,3352]{1,0:T(8,128)}, bf16[192,1024]{1,0:T(8,128)(2,1)}) custom-call(f32[2,768]{1,0:T(2,128)} %refs_0_.9, f32[2,4,1792]{2,1,0:T(4,128)} %refs_1_.8, f32[2,1792]{1,0:T(2,128)} %refs_2_.7, f32[2,24]{1,0:T(2,128)} %refs_3_.7, ...), custom_call_target="tpu_custom_call" | custom-call | tf_op jit(solution)/shard_map/layer_backward_0/pallas_call | solution.py:1084
  267.5 52.4 %finish.1 = (f32[2,96,3352]{2,1,0:T(8,128)}, f32[2,192,768]{2,1,0:T(8,128)}, f32[16,2048]{1,0:T(8,128)}) custom-call(bf16[768,1024]{1,0:T(8,128)(2,1)} %get-tuple-element.75.refs_0_, bf16[1024,3352]{1,0:T(8,128)(2,1)} %get-tuple-element.83.refs_1_, f32[8,2048]{1,0:T(8,128)} %get-tuple-element.84.refs_2_, f32[8,2048]{1,0:T(8,128)} %get-tuple-element.85.refs_3_, ...), custom_call_target="tpu_custom_call" | custom-call | tf_op jit(solution)/shard_map/finish/pallas_call | solution.py:917
  319.8 6.4 %results.1 = (f32[1024,768]{1,0:T(8,128)}, f32[2,96,3352]{2,1,0:T(8,128)}, f32[2,192,768]{2,1,0:T(8,128)}, f32[2,768]{1,0:T(2,128)}, f32[2,4,1792]{2,1,0:T(4,128...) custom-call(f32[16,2048]{1,0:T(8,128)} %get-tuple-element.89.refs_0_, ...), custom_call_target="tpu_custom_call" | custom-call | tf_op jit(solution)/shard_map/results/pallas_call | solution.py:978
